TPU v7x, 512 devices: a whole 4x8x8 slice. The times are simulated.
512 devices in a mesh: mem: 32 (over z, x), tp: 16 (over y, core).
Axes of the slice: x: 4, y: 8, z: 8, core: 2. Of those that a mesh axis runs over, the one named last changes fastest.
Arguments:
- tokens: bfloat16 [12288, 2560], P(('mem', 'tp')), may hold values from -48 to 48
- input_weight: bfloat16 [2560, 6144], P(None, 'tp'), may hold values from -0.125 to 0.125
- output_weight: bfloat16 [2048, 2560], P('tp'), may hold values from -0.125 to 0.125
- gate_logit: float32 [16], P('tp'), may hold values from -2 to 2
- memory: bfloat16 [2, 131072, 2048], P(None, 'mem', 'tp'), may hold values from -48 to 48
- retrieved: int32 [96, 16], P('mem'), may hold values from 0 to 1023, as said below
- block_home: int32 [1024], replicated, may hold values from 0 to 1023, as said below
Outputs:
- mixed: bfloat16 [12288, 2560], P(('mem', 'tp'))
Inputs may be any that keep to these rules, and one draw needn't show every extreme that they name: `block_home`: A permutation: each logical block names one stored block; stored block s lies with index s // 32 of mem, as its block s % 32. `retrieved`: each row names 16 different logical blocks; rows i * 3 to i * 3 + 2 are the query blocks of index i of mem. A row names at most 2 blocks held by one index of mem, and all rows of one index of mem together name at most 2 different blocks held by one index of mem.
All inputs are finite; a program needn't handle non-finite values.
Results may differ from a plain program's by a relative error of at most 0.023.
Values may be sent and summed in bfloat16 or wider, within the bound.
A program may use at most 128 MiB of HBM per device.

v0:
```python
import jax
import jax.numpy as jnp
from jax import lax
from jax.sharding import PartitionSpec as P

HD = 128
BLK = 128
TOPB = 16
CAP = 2


NEG_FILL = -1e30


def from_behind(value, axis, steps):
    count = lax.axis_size(axis)
    initial, last = (max(0, -steps), min(count, count - steps))
    return lax.ppermute(value, axis, [(source, source + steps) for source in range(initial, last)])


def softmax_rows(scores, allowed):
    row_peak = jnp.max(jnp.where(allowed, scores, NEG_FILL), axis=-1, keepdims=True)
    weights = jnp.where(allowed, jnp.exp(scores - row_peak), 0.0)
    return (weights / jnp.sum(weights, axis=-1, keepdims=True)).astype(jnp.bfloat16)


def local(tokens, input_weight, output_weight, gate_logit, memory, retrieved, block_home):
    holder_count = lax.axis_size("mem")
    share_rows = tokens.shape[0]
    local_rows = share_rows * lax.axis_size("tp")
    groups = output_weight.shape[0] // HD
    score_scale = HD ** (-0.5)
    projected = jnp.dot(
        lax.all_gather(tokens, "tp", axis=0, tiled=True),
        input_weight,
        preferred_element_type=jnp.float32,
    )
    projected = projected.astype(jnp.bfloat16).reshape(local_rows, groups, 3, HD)
    queries = projected[:, :, 0]
    key_rows = projected[:, :, 1]
    value_rows = projected[:, :, 2]
    last_rows = jnp.stack([key_rows[-BLK:], value_rows[-BLK:]]).reshape(2, BLK, groups * HD)
    before = from_behind(last_rows, "mem", 1).reshape(2, BLK, groups, HD)
    near_keys = jnp.concatenate([before[0], key_rows], axis=0)
    near_values = jnp.concatenate([before[1], value_rows], axis=0)
    near_scores = (
        jnp.einsum("qgd,kgd->gqk", queries, near_keys, preferred_element_type=jnp.float32)
        * score_scale
    )
    query_index = lax.broadcasted_iota(jnp.int32, (local_rows, local_rows + BLK), 0)
    key_index = lax.broadcasted_iota(jnp.int32, (local_rows, local_rows + BLK), 1)
    first_key = lax.axis_index("mem") * local_rows - BLK
    allowed = (
        (key_index > query_index) & (key_index <= query_index + BLK) & (key_index + first_key >= 0)
    )
    near_probs = softmax_rows(near_scores, allowed[None])
    near_out = jnp.einsum(
        "gqk,kgd->qgd", near_probs, near_values, preferred_element_type=jnp.float32
    )
    blocks_here = retrieved.shape[0]
    entries = blocks_here * TOPB
    local_blocks = memory.shape[1] // BLK
    flat_blocks = retrieved.reshape(entries)
    home_slot = jnp.take(block_home, flat_blocks)
    holder = home_slot // local_blocks
    local_block = home_slot % local_blocks
    local_store = memory.reshape(2, local_blocks, BLK, groups * HD)
    entry_order = jnp.arange(entries)
    earlier = entry_order[None, :] < entry_order[:, None]
    same_owner = holder[:, None] == holder[None, :]
    slot_count = blocks_here * CAP
    slot_of = jnp.sum(same_owner & earlier, axis=1)
    wanted_ids = (
        jnp.zeros((holder_count, slot_count), jnp.int32).at[holder, slot_of].set(local_block)
    )
    picked = jnp.take(
        local_store,
        lax.all_to_all(wanted_ids, "mem", split_axis=0, concat_axis=0, tiled=True),
        axis=1,
    )
    fetched = lax.all_to_all(picked, "mem", split_axis=1, concat_axis=1, tiled=True)
    gathered = fetched[:, holder, slot_of]
    far_pairs = gathered.reshape(2, blocks_here, TOPB * BLK, groups, HD)
    block_queries = queries.reshape(blocks_here, BLK, groups, HD)
    far_scores = (
        jnp.einsum(
            "bqgd,bkgd->bgqk", block_queries, far_pairs[0], preferred_element_type=jnp.float32
        )
        * score_scale
    )
    far_probs = softmax_rows(far_scores, True)
    far_out = jnp.einsum(
        "bgqk,bkgd->bqgd", far_probs, far_pairs[1], preferred_element_type=jnp.float32
    )
    far_out = far_out.reshape(local_rows, groups, HD)
    mixing = jax.nn.sigmoid(gate_logit)[None, :, None]
    attended = (
        (mixing * far_out + (1.0 - mixing) * near_out)
        .astype(jnp.bfloat16)
        .reshape(local_rows, groups * HD)
    )
    return lax.psum_scatter(
        jnp.dot(attended, output_weight, preferred_element_type=jnp.float32).astype(jnp.bfloat16),
        "tp",
        scatter_dimension=0,
        tiled=True,
    )


def solution(mesh):
    placed = (
        P(("mem", "tp"), None),
        P(None, "tp"),
        P("tp", None),
        P("tp"),
        P(None, "mem", "tp"),
        P("mem", None),
        P(),
    )
    return jax.shard_map(
        local, mesh=mesh, in_specs=placed, out_specs=P(("mem", "tp"), None), check_vma=False
    )
```

profile of v0, /device:TPU:4, one launch (start us, length us, event | category | flops | bytes accessed | tf_op | source)
XLA Modules:
  0.0 451.7 jit_solution(2877653333956083581)
XLA Ops:
  6.5 0.9 reshape.326
  7.4 0.8 reshape.327
  8.2 1.5 gather_fusion
  9.7 0.2 convert_reduce_fusion
  10.0 2.8 scatter_fusion
  12.8 20.9 %all_to_all.20 = s32[32,1,6]{2,1,0:T(1,128)S(1)} all-to-all(s32[32,1,6]{2,1,0:T(1,128)S(1)} %copy.27), channel_id=1, replica_groups=mesh['mem'=32,'tp'=16] {'mem'}, dimensions={0} | all-to-all | bytes 1536 | tf_op jit(solution)/shard_map/all_to_all | solution.py:78
  34.0 7.8 %gather_fusion.1 = bf16[192,2,128,128]{3,2,1,0:T(8,128)(2,1)} fusion(bf16[2,32,128,128]{3,2,1,0:T(8,128)(2,1)S(1)} %bitcast.95, s32[1024]{0:T(1024)S(1)} %pad_clamp_fusion), kind=kCustom, calls=%fused_computation.1 | custom fusion | bytes 25166592 | tf_op jit(solution)/shard_map/jit(_take)/gather | solution.py:76
  41.8 10.8 %fusion.1 = bf16[2,32,6,128,128]{4,3,2,0,1:T(8,128)(2,1)} fusion(bf16[32,6,2,128,128]{4,3,2,1,0:T(8,128)(2,1)} %bitcast.97, pred[32,6]{1,0:T(8,128)(4,1)S(1)} %copy.29), kind=kLoop, calls=%fused_computation.6 | loop fusion | flops 6291456 | bytes 25166016 | tf_op jit(solution)/shard_map/jit(_take)/select_n | solution.py:76
  52.6 6.8 %all-to-all-start.1 = ((bf16[2,32,6,128,128]{4,3,2,0,1:T(8,128)(2,1)}), bf16[2,32,6,128,128]{4,3,2,0,1:T(8,128)(2,1)}, u32[]{:S(2)}, u32[]{:S(2)}) async-start(bf16[2,32,6,128,128]{4,3,2,0,1:T(8,128)(2,1)} %fusion.1), calls=%async_computation.1 | async-start | bytes 25165824 | tf_op jit(solution)/shard_map/all_to_all | solution.py:81
  59.5 0.7 all-gather.2.cloned.1.call-update
  61.0 44.3 %all-gather.2.cloned.1.call-done = bf16[384,2560]{1,0:T(8,128)(2,1)} async-done(((bf16[24,2560]{1,0:T(8,128)(2,1)}), bf16[384,2560]{1,0:T(8,128)(2,1)}) %all-gather.2.cloned.1.call-update) | async-done | bytes 1966096 | tf_op jit(solution)/shard_map/all_gather | solution.py:34
  105.3 3.4 convolution_convert_fusion.1
  108.7 3.1 collective-permute-start
  111.9 3.4 collective-permute-done
  115.4 0.4 select_reduce_fusion
  115.8 0.4 fusion.12
  116.2 221.0 %all-to-all-done.1 = bf16[2,32,6,128,128]{4,3,2,0,1:T(8,128)(2,1)} async-done(((bf16[2,32,6,128,128]{4,3,2,0,1:T(8,128)(2,1)}), bf16[2,32,6,128,128]{4,3,2,0,1:T(8,128)(2,1)}, u32[]{:S(2)}, u32[]{:S(2)}) %all-to-all-start.1) | async-done | bytes 12582944 | tf_op jit(solution)/shard_map/all_to_all | solution.py:81
  337.2 11.9 %copy.31 = bf16[2,32,6,128,128]{4,3,2,1,0:T(8,128)(2,1)} copy(bf16[2,32,6,128,128]{4,3,2,0,1:T(8,128)(2,1)} %all-to-all-done.1) | data formatting | bytes 25165824 | tf_op jit(solution)/shard_map/all_to_all | solution.py:81
  349.1 7.4 %gather_fusion.2 = bf16[48,2,128,128]{3,2,1,0:T(8,128)(2,1)} fusion(bf16[2,32,6,128,128]{4,3,2,1,0:T(8,128)(2,1)} %copy.31, s32[48]{0:T(128)S(1)} %get-tuple-element.5), kind=kCustom, calls=%fused_computation.2 | custom fusion | bytes 6291840 | tf_op jit(solution)/shard_map/gather | solution.py:82
  356.5 3.4 fusion.42
  359.9 2.7 fusion.43
  362.6 3.0 fusion.6
  365.7 3.7 convolution_convert_fusion
  369.5 75.4 %reduce-scatter.2.cloned.1.call-done = bf16[24,2560]{1,0:T(8,128)(2,1)} async-done(((bf16[384,2560]{1,0:T(8,128)(2,1)}), bf16[24,2560]{1,0:T(8,128)(2,1)}) %reduce-scatter.2.cloned.1.call-update) | async-done | bytes 122896 | tf_op jit(solution)/shard_map/reduce_scatter | solution.py:102
  (29 shorter events, 0.9 us)
Async XLA Ops:
  6.5 27.5 %copy-start = (bf16[2,4096,128]{2,1,0:T(8,128)(2,1)S(1)}, bf16[2,4096,128]{2,1,0:T(8,128)(2,1)}, u32[]{:S(2)}) copy-start(bf16[2,4096,128]{2,1,0:T(8,128)(2,1)} %param.11) | copy-start | bytes 6291460
  52.6 284.6 %all-to-all-start.1 = ((bf16[2,32,6,128,128]{4,3,2,0,1:T(8,128)(2,1)}), bf16[2,32,6,128,128]{4,3,2,0,1:T(8,128)(2,1)}, u32[]{:S(2)}, u32[]{:S(2)}) async-start(bf16[2,32,6,128,128]{4,3,2,0,1:T(8,128)(2,1)} %fusion.1), calls=%async_computation.1 | async-start | bytes 25165824 | tf_op jit(solution)/shard_map/all_to_all | solution.py:81
  59.5 45.8 %all-gather.2.cloned.1.call-start = ((), (), s32[]{:S(2)}) async-start(), calls=%async_computation.3 | async-start | bytes 2088960 | tf_op jit(solution)/shard_map/all_gather | solution.py:34
  60.2 384.7 %reduce-scatter.2.cloned.1.call-start = ((), (), s32[]{:S(2)}) async-start(), calls=%async_computation.4 | async-start | bytes 2088960 | tf_op jit(solution)/shard_map/reduce_scatter | solution.py:102
  108.7 6.7 %collective-permute-start = (bf16[2,128,128]{1,2,0:T(8,128)(2,1)S(1)}, bf16[2,128,128]{1,2,0:T(8,128)(2,1)S(1)}, u32[]{:S(2)}, u32[]{:S(2)}) collective-permute-start(bf16[2,128,128]{1,2,0:T(8,128)(2,1)S(1)} %maximum_bitcast_fusion.5), channel_id=1, source_target_pairs={{0,16},{16,32},{32,48},{48,64},{64,80},{80,96},{96,112},{112,128},... | collective-permute-start | bytes 196616 | tf_op jit(solution)/shard_map/ppermute | solution.py:18
  365.7 79.1 %copy-start.1 = (bf16[2,4096,128]{2,1,0:T(8,128)(2,1)S(1)}, bf16[2,4096,128]{2,1,0:T(8,128)(2,1)}, u32[]{:S(2)}) copy-start(bf16[2,4096,128]{2,1,0:T(8,128)(2,1)} %param.11) | copy-start | bytes 6291460
Sparse Core Ops, SparseCore 0:
  62.4 42.8 all-gather.1
  369.6 75.2 reduce-scatter.1
where the time goes:
time: 452 us
  waiting for transfers between devices  345 us (76%)
  local copies, waits for them, and re-layouts  37.1 us (8%)
  blocking collectives  20.9 us (5%)
  between operations  14.3 us (3%)
  matrix products  13.2 us (3%)
  other arithmetic  11.5 us (3%)
  starting transfers between devices  9.97 us (2%)
    all_to_all x1, waiting for transfers between devices, local(): lax.all_to_all(picked, 'mem', split_axis=1, concat_axis=1, tiled=True)  221 us
    reduce_scatter x1, waiting for transfers between devices, local(): lax.psum_scatter(jnp.dot(attended, output_weight, preferred_element_type=...  75.4 us
    all_gather x1, waiting for transfers between devices, local(): lax.all_gather(tokens, 'tp', axis=0, tiled=True)  44.3 us
    all_to_all x1, blocking collectives, local(): lax.all_to_all(wanted_ids, 'mem', split_axis=0, concat_axis=0, tiled=True)  20.9 us
    all_to_all x1, local copies, waits for them, and re-layouts, local(): lax.all_to_all(picked, 'mem', split_axis=1, concat_axis=1, tiled=True)  11.9 us
    select_n x2, other arithmetic, local(): jnp.take(local_store, lax.all_to_all(wanted_ids, 'mem', split_axis=0, con...  10.8 us
  transfers between devices with their start and end apart: 4, of which 4 were waited for; matrix products, arithmetic and copies ran while one was open for 1% of the time, Pallas kernels for 0%

commit v1 on v0

v1 whole, which is shorter than its diff:
```python
import functools

import jax
import jax.numpy as jnp
from jax import lax
from jax.experimental import pallas as pl
from jax.experimental.pallas import tpu as pltpu
from jax.sharding import PartitionSpec as P

HD = 128
BLK = 128
XS = 4
RING = 8
MESH = pl.DeviceIdType.MESH
NONE = -1e30
BF16 = jnp.bfloat16
F32 = jnp.float32


def ring_offset(step):
    half = step // 2
    even = lax.rem(step, 2) == 0 if not isinstance(step, int) else step % 2 == 0
    if isinstance(step, int):
        return (4 - half) if even else (half - 3)
    return jnp.where(even, 4 - half, half - 3)


def kernel(
    tok_ref, rec_ref, gate_ref, wi_hbm, wo_hbm, mem_hbm, out_ref,
    tok_all, x_all, wi_v, wo_v, mem_v,
    flags_v, stage_v, table_v, flags_s, table_s,
    kv_send, kv_all, q_all, keys_v, vals_v, halo,
    near_v, far_v, lse_v, o_send, o_recv, l_send, l_recv,
    part, sib_part, y_send, y_recv,
    in_sem,
    tr_s, tr_r, tl_s, tl_r, ts_s, ts_r,
    fz_s, fz_r, fx_s, fx_r, sm_sem,
    kv_s, kv_r, qr_s, qr_r, ql_s, ql_r, h_s, h_r,
    o_s, o_r, l_s, l_r, ps_s, ps_r, y_s, y_r,
):
    m = lax.axis_index("mem")
    t = lax.axis_index("tp")
    z, x = m // XS, lax.rem(m, XS)
    y, c = t // 2, lax.rem(t, 2)
    sibling = (m, t + 1 - 2 * c)
    y_up = (m, lax.rem(y + 1, RING) * 2 + c)
    y_down = (m, lax.rem(y + RING - 1, RING) * 2 + c)
    z_up = (lax.rem(z + 1, RING) * XS + x, t)
    z_down = (lax.rem(z + RING - 1, RING) * XS + x, t)
    nmem = RING * XS
    following = (lax.rem(m + 1, nmem), t)
    preceding = (lax.rem(m + nmem - 1, nmem), t)

    def x_peer(d):
        return (z * XS + lax.rem(x + d, XS), t)

    def z_peer(d):
        return (lax.rem(z + d, RING) * XS + x, t)

    def send(src, dst, s, r, to):
        return pltpu.make_async_remote_copy(
            src_ref=src, dst_ref=dst, send_sem=s, recv_sem=r, device_id=to, device_id_type=MESH
        )

    loads = [
        pltpu.make_async_copy(mem_hbm, mem_v, in_sem.at[0]),
        pltpu.make_async_copy(wi_hbm, wi_v, in_sem.at[1]),
        pltpu.make_async_copy(wo_hbm, wo_v, in_sem.at[2]),
    ]
    for load in loads:
        load.start()

    barrier = pltpu.get_barrier_semaphore()
    partners = [sibling, y_up, y_down, following, preceding]
    partners += [x_peer(d) for d in range(1, XS)] + [z_peer(d) for d in range(1, RING)]
    for to in partners:
        pl.semaphore_signal(barrier, inc=1, device_id=to, device_id_type=MESH)

    own = tok_ref[...].astype(F32)
    half = own.shape[1] // 2
    rows = own.shape[0]
    tok_all[y, c] = jnp.concatenate([own[:, :half], own[:, half:]], axis=0).astype(BF16)
    flags_v[z] = rec_ref[z]

    pl.semaphore_wait(barrier, len(partners))

    flag_copies = [
        send(rec_ref.at[lax.rem(z + d, RING)], flags_v.at[z], fz_s.at[d - 1], fz_r.at[d - 1], z_peer(d))
        for d in range(1, RING)
    ]

    def flag_arrival(d):
        at = lax.rem(z + RING - d, RING)
        return send(flags_v.at[at], flags_v.at[at], fz_s.at[d - 1], fz_r.at[d - 1], z_peer(d))

    for copy in flag_copies:
        copy.start()

    def ring_right(ref, k, s, r, to, me):
        at = lax.rem(me + RING - k, RING)
        return send(ref(at), ref(at), s.at[k], r.at[k], to)

    def ring_left(ref, k, s, r, to, me):
        at = lax.rem(me + k, RING)
        return send(ref(at), ref(at), s.at[k], r.at[k], to)

    def tok_at(at):
        return tok_all.at[at, c]

    def tok_right(k):
        return ring_right(tok_at, k, tr_s, tr_r, y_up, y)

    def tok_left(k):
        return ring_left(tok_at, k, tl_s, tl_r, y_down, y)

    def tok_sib(k, at):
        return send(tok_all.at[at, c], tok_all.at[at, c], ts_s.at[k], ts_r.at[k], sibling)

    def right_recv(ref, k, s, r, to, me):
        at = lax.rem(me + RING - k - 1, RING)
        send(ref(at), ref(at), s.at[k], r.at[k], to).wait_recv()

    def left_recv(ref, k, s, r, to, me):
        at = lax.rem(me + k + 1, RING)
        send(ref(at), ref(at), s.at[k], r.at[k], to).wait_recv()

    def tok_place(offset):
        return lax.rem(y + offset + RING, RING)

    order = [0, -1, 1, -2, 2, -3, 3, -4]
    tok_right(0).start()
    tok_left(0).start()
    tok_sib(0, y).start()

    def tok_step(k):
        right_recv(tok_at, k, tr_s, tr_r, y_up, y)
        if k < 3:
            tok_right(k + 1).start()
        tok_sib(2 * k + 1, tok_place(-k - 1)).start()
        if k < 3:
            left_recv(tok_at, k, tl_s, tl_r, y_down, y)
            if k < 2:
                tok_left(k + 1).start()
            tok_sib(2 * k + 2, tok_place(k + 1)).start()

    for d in range(1, RING):
        flag_arrival(d).wait_recv()
    for d in range(XS):
        stage_v[d] = flags_v[:, lax.rem(x + d, XS)]
    table_copies = [
        send(stage_v.at[d], table_v.at[d], fx_s.at[d - 1], fx_r.at[d - 1], x_peer(d)) for d in range(1, XS)
    ]
    for copy in table_copies:
        copy.start()
    table_v[0] = stage_v[0]
    flags_to_s = pltpu.make_async_copy(flags_v, flags_s, sm_sem.at[0])
    flags_to_s.start()
    for copy in table_copies:
        copy.wait_recv()
    table_to_s = pltpu.make_async_copy(table_v, table_s, sm_sem.at[1])
    table_to_s.start()
    loads[0].wait()
    table_to_s.wait()
    tok_step(0)

    def kv_copy(d, i):
        return send(kv_send.at[d - 1, i], kv_all.at[d, i], kv_s.at[d - 1, i], kv_r.at[d - 1, i], x_peer(d))

    def pack(i, carry):
        zr = lax.rem(z + ring_offset(i) + RING, RING)
        for d in (2, 1, 3, 0):
            for slot in range(2):
                block = table_s[(XS - d) % XS, zr, 0, slot]
                key = mem_v[0, block]
                value = mem_v[1, block].astype(F32).T.astype(BF16)
                if d:
                    kv_send[d - 1, i, slot] = key
                    kv_send[d - 1, i, 2 + slot] = value
                else:
                    kv_all[0, i, slot] = key
                    kv_all[0, i, 2 + slot] = value
            if d:
                kv_copy(d, i).start()
        return carry

    lax.fori_loop(0, 4, pack, 0)
    tok_step(1)
    lax.fori_loop(4, 8, pack, 0)
    tok_step(2)
    tok_step(3)
    flags_to_s.wait()
    loads[1].wait()

    for k in range(RING):
        at = tok_place(order[k])
        theirs = tok_all.at[at, 1 - c]
        send(theirs, theirs, ts_s.at[k], ts_r.at[k], sibling).wait_recv()
        a = tok_all[at, 0].astype(F32)
        b = tok_all[at, 1].astype(F32)
        left = jnp.concatenate([a[:rows], b[:rows]], axis=0)
        right = jnp.concatenate([a[rows:], b[rows:]], axis=0)
        x_all[pl.ds(pl.multiple_of(at * 2 * rows, 16), 2 * rows), :] = jnp.concatenate(
            [left, right], axis=1
        ).astype(BF16)

    projected = jnp.dot(x_all[...], wi_v[...], preferred_element_type=F32)
    q_all[z] = projected[:, :HD].T.astype(BF16)
    keys_v[...] = projected[:, HD : 2 * HD].astype(BF16)
    vals_v[...] = projected[:, 2 * HD :].T.astype(BF16)

    def q_at(at):
        return q_all.at[at]

    def q_right(k):
        return ring_right(q_at, k, qr_s, qr_r, z_up, z)

    def q_left(k):
        return ring_left(q_at, k, ql_s, ql_r, z_down, z)

    def q_step(k):
        right_recv(q_at, k, qr_s, qr_r, z_up, z)
        if k < 3:
            q_right(k + 1).start()
            left_recv(q_at, k, ql_s, ql_r, z_down, z)
            if k < 2:
                q_left(k + 1).start()

    q_right(0).start()
    q_left(0).start()
    blocks = keys_v.shape[0] // BLK
    last = (blocks - 1) * BLK
    halo_copies = [
        send(keys_v.at[pl.ds(last, BLK)], halo.at[0], h_s.at[0], h_r.at[0], following),
        send(vals_v.at[:, pl.ds(last, BLK)], halo.at[1], h_s.at[1], h_r.at[1], following),
    ]
    for copy in halo_copies:
        copy.start()

    unit = HD ** (-0.5) * 1.4426950408889634

    key_row = lax.broadcasted_iota(jnp.int32, (BLK, BLK), 0)
    query_col = lax.broadcasted_iota(jnp.int32, (BLK, BLK), 1)

    def near(j):
        cols = slice(j * BLK, (j + 1) * BLK)
        query = q_all[z, :, cols]
        if j == 0:
            key0, val0 = halo[0], halo[1]
            seen = jnp.where(m > 0, 0.0, NONE).astype(F32)
        else:
            key0 = keys_v[(j - 1) * BLK : j * BLK, :]
            val0 = vals_v[:, (j - 1) * BLK : j * BLK]
            seen = None
        s0 = jnp.dot(key0, query, preferred_element_type=F32) * unit
        s1 = jnp.dot(keys_v[cols, :], query, preferred_element_type=F32) * unit
        s0 = jnp.where(key_row > query_col, s0, NONE)
        s1 = jnp.where(key_row <= query_col, s1, NONE)
        if seen is not None:
            s0 = s0 + seen
        peak = jnp.maximum(jnp.max(s0, axis=0, keepdims=True), jnp.max(s1, axis=0, keepdims=True))
        p0 = jnp.exp2(s0 - peak)
        p1 = jnp.exp2(s1 - peak)
        total = jnp.sum(p0, axis=0, keepdims=True) + jnp.sum(p1, axis=0, keepdims=True)
        o = jnp.dot(val0, p0.astype(BF16), preferred_element_type=F32)
        o = o + jnp.dot(vals_v[:, cols], p1.astype(BF16), preferred_element_type=F32)
        near_v[:, cols] = o * (1.0 / total)

    q_step(0)
    near(1)
    q_step(1)
    near(2)
    q_step(2)
    for copy in halo_copies:
        copy.wait_recv()
    near(0)
    q_step(3)

    def o_copies(i, to):
        return (
            send(o_send.at[i], o_recv.at[i], o_s.at[i], o_r.at[i], to),
            send(l_send.at[i], l_recv.at[i], l_s.at[i], l_r.at[i], to),
        )

    def merge(i):
        for copy in o_copies(i, z_up):
            copy.wait_recv()
        la, lb = lse_v[0:1, :], l_recv[i][0:1, :]
        top = jnp.maximum(la, lb)
        wa, wb = jnp.exp2(la - top), jnp.exp2(lb - top)
        total = wa + wb
        inverse = 1.0 / total
        far_v[...] = (wa * inverse) * far_v[...] + (wb * inverse) * o_recv[i].astype(F32)
        lse_v[...] = jnp.broadcast_to(top + jnp.log2(total), lse_v.shape)

    def attend(i, carry):
        zr = lax.rem(z + ring_offset(i) + RING, RING)
        for d in range(1, XS):
            kv_copy(d, i).wait_recv()
        for j in range(blocks):
            cols = slice(j * BLK, (j + 1) * BLK)
            query = q_all[zr, :, cols]
            scores = []
            peak = None
            for d in range(XS):
                holder = lax.rem(x + XS - d, XS)
                keys = kv_all[d, i, 0:2].reshape(2 * BLK, HD)
                s = jnp.dot(keys, query, preferred_element_type=F32) * unit
                for slot in range(2):
                    flag = flags_s[zr, holder, 0, 2 + 2 * j + slot].astype(F32)
                    one = s[slot * BLK : (slot + 1) * BLK] + (flag - 1.0) * (-NONE)
                    scores.append(one)
                    high = jnp.max(one, axis=0, keepdims=True)
                    peak = high if peak is None else jnp.maximum(peak, high)
            total = None
            o = None
            for d in range(XS):
                p = [jnp.exp2(scores[2 * d + slot] - peak) for slot in range(2)]
                count = jnp.sum(p[0] + p[1], axis=0, keepdims=True)
                total = count if total is None else total + count
                probs = jnp.concatenate([p[0].astype(BF16), p[1].astype(BF16)], axis=0)
                vals = jnp.concatenate([kv_all[d, i, 2], kv_all[d, i, 3]], axis=1)
                term = jnp.dot(vals, probs, preferred_element_type=F32)
                o = term if o is None else o + term
            far_v[:, cols] = o * (1.0 / total)
            lse_v[:, cols] = jnp.broadcast_to(peak + jnp.log2(total), (8, BLK))

        @pl.when(i >= 2)
        def _():
            merge(i - 2)

        @pl.when(i < 7)
        def _():
            up = lax.rem(i, 2) == 0
            to = (jnp.where(up, z_up[0], z_down[0]), t)
            o_send[i] = far_v[...].astype(BF16)
            l_send[i] = lse_v[...]
            for copy in o_copies(i, to):
                copy.start()

        return carry

    lax.fori_loop(0, 8, attend, 0)
    merge(6)

    share = 1.0 / (1.0 + jnp.exp(jnp.full((1, HD), -gate_ref[0], F32)))
    share = share[:, 0:1]
    attended = (share * far_v[...] + (1.0 - share) * near_v[...]).T.astype(BF16)
    loads[2].wait()
    width = 256

    def project_out(n, carry):
        at_left = pl.multiple_of(n * width, width)
        at_right = pl.multiple_of(half + n * width, width)
        left = jnp.dot(attended, wo_v[:, pl.ds(at_left, width)], preferred_element_type=F32)
        right = jnp.dot(attended, wo_v[:, pl.ds(at_right, width)], preferred_element_type=F32)
        for k in range(2 * RING):
            part[k, :, pl.ds(at_left, width)] = jnp.concatenate(
                [left[k * rows : (k + 1) * rows], right[k * rows : (k + 1) * rows]], axis=0
            ).astype(BF16)
        return carry

    lax.fori_loop(0, half // width, project_out, 0)

    def y_place(i):
        return lax.rem(y + ring_offset(i) + RING, RING)

    def part_copy(i):
        return send(part.at[2 * y_place(i) + 1 - c], sib_part.at[i], ps_s.at[i], ps_r.at[i], sibling)

    for i in range(RING):
        part_copy(i).start()

    def y_copy(i):
        return send(y_send.at[i], y_recv.at[i], y_s.at[i], y_r.at[i], y_up if i % 2 == 0 else y_down)

    for i in range(RING):
        part_copy(i).wait_recv()
        total = part[2 * y_place(i) + c].astype(F32) + sib_part[i].astype(F32)
        if i >= 2:
            y_copy(i - 2).wait_recv()
            total = total + y_recv[i - 2].astype(F32)
        if i < 7:
            y_send[i] = total.astype(BF16)
            y_copy(i).start()
        else:
            y_copy(6).wait_recv()
            total = total + y_recv[6].astype(F32)
            out_ref[...] = jnp.concatenate([total[:rows], total[rows:]], axis=1).astype(BF16)

    for copy in flag_copies + table_copies + halo_copies:
        copy.wait_send()
    for k in range(4):
        tok_right(k).wait_send()
        q_right(k).wait_send()
    for k in range(3):
        tok_left(k).wait_send()
        q_left(k).wait_send()
    for k in range(RING):
        tok_sib(k, tok_place(order[k])).wait_send()
        part_copy(k).wait_send()
    for i in range(7):
        for copy in o_copies(i, z_up):
            copy.wait_send()
        y_copy(i).wait_send()

    def kv_sent(i, carry):
        for d in range(1, XS):
            kv_copy(d, i).wait_send()
        return carry

    lax.fori_loop(0, 8, kv_sent, 0)


def requests(retrieved, block_home, owners, blocks_per_owner):
    rows, entries = retrieved.shape
    every = jnp.arange(block_home.shape[0], dtype=jnp.int32)
    home = jnp.sum(jnp.where(retrieved[:, :, None] == every, block_home[None, None, :], 0), axis=-1)
    named = jnp.any(home[:, :, None] == every, axis=1).reshape(rows, owners, blocks_per_owner)
    local_id = jnp.arange(blocks_per_owner, dtype=jnp.int32)
    anyone = jnp.any(named, axis=0)
    first = jnp.min(jnp.where(anyone, local_id, blocks_per_owner - 1), axis=-1)
    second = jnp.max(jnp.where(anyone, local_id, 0), axis=-1)
    of_first = jnp.any(named & (local_id == first[:, None]), axis=-1)
    of_second = jnp.any(named & (local_id == second[:, None]), axis=-1) & (second != first)
    flags = jnp.stack([of_first, of_second], axis=-1).astype(jnp.int32)
    flags = jnp.transpose(flags, (1, 0, 2)).reshape(owners, 2 * rows)
    record = jnp.concatenate([first[:, None], second[:, None], flags], axis=1)
    record = jnp.pad(record, ((0, 0), (0, 128 - record.shape[1])))
    return record.reshape(RING, XS, 1, 128)


def local(tokens, input_weight, output_weight, gate_logit, memory, retrieved, block_home):
    rows, width = tokens.shape
    store = memory.reshape(2, memory.shape[1] // BLK, BLK, HD)
    span = rows * 2 * RING
    record = requests(retrieved, block_home, RING * XS, memory.shape[1] // BLK)
    vmem = pltpu.VMEM
    dma = pltpu.SemaphoreType.DMA
    packed = (2 * rows, width // 2)
    scratch = [
        vmem((RING, 2) + packed, BF16),
        vmem((span, width), BF16),
        vmem(input_weight.shape, BF16),
        vmem(output_weight.shape, BF16),
        vmem(store.shape, BF16),
        vmem((RING, XS, 1, 128), jnp.int32),
        vmem((XS, RING, 1, 128), jnp.int32),
        vmem((XS, RING, 1, 128), jnp.int32),
        pltpu.SMEM((RING, XS, 1, 128), jnp.int32),
        pltpu.SMEM((XS, RING, 1, 128), jnp.int32),
        vmem((XS - 1, RING, 4, BLK, HD), BF16),
        vmem((XS, RING, 4, BLK, HD), BF16),
        vmem((RING, HD, span), BF16),
        vmem((span, HD), BF16),
        vmem((HD, span), BF16),
        vmem((2, BLK, HD), BF16),
        vmem((HD, span), F32),
        vmem((HD, span), F32),
        vmem((8, span), F32),
        vmem((7, HD, span), BF16),
        vmem((7, HD, span), BF16),
        vmem((7, 8, span), F32),
        vmem((7, 8, span), F32),
        vmem((2 * RING,) + packed, BF16),
        vmem((RING,) + packed, BF16),
        vmem((7,) + packed, BF16),
        vmem((7,) + packed, BF16),
        dma((3,)),
        dma((4,)), dma((4,)), dma((3,)), dma((3,)), dma((8,)), dma((8,)),
        dma((7,)), dma((7,)), dma((3,)), dma((3,)), dma((2,)),
        dma((3, 8)), dma((3, 8)), dma((4,)), dma((4,)), dma((3,)), dma((3,)), dma((2,)), dma((2,)),
        dma((7,)), dma((7,)), dma((7,)), dma((7,)), dma((8,)), dma((8,)), dma((7,)), dma((7,)),
    ]
    whole = pl.BlockSpec(memory_space=pltpu.VMEM)
    outside = pl.BlockSpec(memory_space=pl.ANY)
    return pl.pallas_call(
        kernel,
        out_shape=jax.ShapeDtypeStruct(tokens.shape, BF16),
        in_specs=[whole, whole, pl.BlockSpec(memory_space=pltpu.SMEM), outside, outside, outside],
        out_specs=whole,
        scratch_shapes=scratch,
        compiler_params=pltpu.CompilerParams(
            collective_id=0, has_side_effects=True, vmem_limit_bytes=56 * 2**20
        ),
    )(tokens, record, gate_logit, input_weight, output_weight, store)


def solution(mesh):
    placed = (
        P(("mem", "tp"), None),
        P(None, "tp"),
        P("tp", None),
        P("tp"),
        P(None, "mem", "tp"),
        P("mem", None),
        P(),
    )
    return jax.shard_map(
        local, mesh=mesh, in_specs=placed, out_specs=P(("mem", "tp"), None), check_vma=False
    )
```

time: 452 us -> 115 us (0.25)
  the two profiles are of different devices: /device:TPU:4 before, /device:TPU:2 now
where the time goes in v1:
time: 115 us
  Pallas kernels  111 us (97%)
  local copies, waits for them, and re-layouts  2.43 us (2%)
  other arithmetic  1.48 us (1%)
    pallas_call x1, Pallas kernels, local(): pl.pallas_call(kernel, out_shape=jax.ShapeDtypeStruct(tokens.shape, BF16)...  111 us

profile of v1, /device:TPU:2, one launch (start us, length us, event | category | flops | bytes accessed | tf_op | source)
XLA Modules:
  0.0 115.2 jit_solution(1614682949558336307)
XLA Ops:
  0.7 0.9 select_reduce_fusion
  1.6 0.1 fusion.1
  1.7 0.1 reduce_or.41
  1.8 0.1 select_reduce_fusion.2
  1.9 0.1 iota_compare_fusion.2
  2.0 0.1 reshape.86
  2.1 0.2 and_reduce_fusion.1
  2.4 0.1 copy.14
  2.4 0.6 pad.4.clone
  3.1 110.6 %shard_map.73 = bf16[24,2560]{1,0:T(8,128)(2,1)} custom-call(bf16[24,2560]{1,0:T(8,128)(2,1)} %tok_ref.1, s32[8,4,1,128]{3,2,1,0:T(1,128)} %bitcast.12, f32[1]{0:T(128)S(6)} %copy.16.gate_ref, bf16[2560,384]{1,0:T(8,128)(2,1)} %wi_hbm.1, bf16[128,2560]{1,0:T(8,128)(2,1)} %wo_hbm.1, bf16[2,32,128,128]{3,2,1,0:T(8,128)(2,1)} %bitcast.11), custom_call_target="tpu_custom_call" | custom-call | tf_op jit(solution)/shard_map/pallas_call | solution.py:476
  113.6 1.6 %copy.17 = bf16[24,2560]{1,0:T(8,128)(2,1)} copy(bf16[24,2560]{1,0:T(8,128)(2,1)} %shard_map.73) | data formatting | bytes 245760
  (6 shorter events, 0.0 us)

commit v2 on v1

--- a/solution.py
+++ b/solution.py
@@ -26,36 +26,38 @@
 
 
 def kernel(
-    tok_ref, rec_ref, gate_ref, wi_hbm, wo_hbm, mem_hbm, out_ref,
-    tok_all, x_all, wi_v, wo_v, mem_v,
-    flags_v, stage_v, table_v, flags_s, table_s,
+    ret_ref, home_ref, gate_ref, tok_ref, wi_hbm, wo_hbm, mem_hbm, out_ref,
+    tok_all, x_all, wi_v, wo_all, mem_v,
+    rec_v, table_v, table_s,
     kv_send, kv_all, q_all, keys_v, vals_v, halo,
     near_v, far_v, lse_v, o_send, o_recv, l_send, l_recv,
-    part, sib_part, y_send, y_recv,
+    att_v, att_send, att_all, part, y_send, y_recv,
     in_sem,
-    tr_s, tr_r, tl_s, tl_r, ts_s, ts_r,
-    fz_s, fz_r, fx_s, fx_r, sm_sem,
+    tr_s, tr_r, tl_s, tl_r, ts_s, ts_r, rec_s, rec_r,
     kv_s, kv_r, qr_s, qr_r, ql_s, ql_r, h_s, h_r,
-    o_s, o_r, l_s, l_r, ps_s, ps_r, y_s, y_r,
+    o_s, o_r, l_s, l_r, w_s, w_r, a_s, a_r, y_s, y_r,
 ):
     m = lax.axis_index("mem")
     t = lax.axis_index("tp")
     z, x = m // XS, lax.rem(m, XS)
     y, c = t // 2, lax.rem(t, 2)
-    sibling = (m, t + 1 - 2 * c)
-    y_up = (m, lax.rem(y + 1, RING) * 2 + c)
-    y_down = (m, lax.rem(y + RING - 1, RING) * 2 + c)
+    nmem = RING * XS
+
+    def at_y(where, core):
+        return (m, lax.rem(where + RING, RING) * 2 + core)
+
+    sibling = at_y(y, 1 - c)
+    y_up, y_down = at_y(y + 1, c), at_y(y - 1, c)
+    across, across_other = at_y(y + 4, c), at_y(y + 4, 1 - c)
     z_up = (lax.rem(z + 1, RING) * XS + x, t)
     z_down = (lax.rem(z + RING - 1, RING) * XS + x, t)
-    nmem = RING * XS
     following = (lax.rem(m + 1, nmem), t)
-    preceding = (lax.rem(m + nmem - 1, nmem), t)
+
+    def mem_peer(d):
+        return (lax.rem(m + d, nmem), t)
 
     def x_peer(d):
         return (z * XS + lax.rem(x + d, XS), t)
-
-    def z_peer(d):
-        return (lax.rem(z + d, RING) * XS + x, t)
 
     def send(src, dst, s, r, to):
         return pltpu.make_async_remote_copy(
@@ -65,36 +67,51 @@
     loads = [
         pltpu.make_async_copy(mem_hbm, mem_v, in_sem.at[0]),
         pltpu.make_async_copy(wi_hbm, wi_v, in_sem.at[1]),
-        pltpu.make_async_copy(wo_hbm, wo_v, in_sem.at[2]),
+        pltpu.make_async_copy(wo_hbm, wo_all.at[0], in_sem.at[2]),
     ]
+
+    barrier = pltpu.get_barrier_semaphore()
+    partners = [sibling, y_up, y_down, across, across_other]
+    for to in partners:
+        pl.semaphore_signal(barrier, inc=1, device_id=to, device_id_type=MESH)
+
+    def greet(d, carry):
+        pl.semaphore_signal(barrier, inc=1, device_id=mem_peer(d), device_id_type=MESH)
+        return carry
+
+    lax.fori_loop(1, nmem, greet, 0)
     for load in loads:
         load.start()
-
-    barrier = pltpu.get_barrier_semaphore()
-    partners = [sibling, y_up, y_down, following, preceding]
-    partners += [x_peer(d) for d in range(1, XS)] + [z_peer(d) for d in range(1, RING)]
-    for to in partners:
-        pl.semaphore_signal(barrier, inc=1, device_id=to, device_id_type=MESH)
 
     own = tok_ref[...].astype(F32)
     half = own.shape[1] // 2
     rows = own.shape[0]
     tok_all[y, c] = jnp.concatenate([own[:, :half], own[:, half:]], axis=0).astype(BF16)
-    flags_v[z] = rec_ref[z]
-
-    pl.semaphore_wait(barrier, len(partners))
-
-    flag_copies = [
-        send(rec_ref.at[lax.rem(z + d, RING)], flags_v.at[z], fz_s.at[d - 1], fz_r.at[d - 1], z_peer(d))
-        for d in range(1, RING)
-    ]
-
-    def flag_arrival(d):
-        at = lax.rem(z + RING - d, RING)
-        return send(flags_v.at[at], flags_v.at[at], fz_s.at[d - 1], fz_r.at[d - 1], z_peer(d))
-
-    for copy in flag_copies:
-        copy.start()
+
+    lane = lax.broadcasted_iota(jnp.int32, (RING, 128), 1)
+    place = lax.broadcasted_iota(jnp.int32, (RING, 128), 0) * 128 + lane
+    number = lax.rem(lane, 32)
+    names = jnp.zeros((RING, 128), jnp.int32)
+    blocks, entries = ret_ref.shape
+    for j in range(blocks):
+        hit = jnp.zeros((RING, 128), jnp.int32)
+        for e in range(entries):
+            hit = jnp.where(place == home_ref[ret_ref[j, e]], 1, hit)
+        names = names + hit * (1 << j)
+    word = number * 8 + names
+    low = jnp.where(names > 0, word, 31 * 8)
+    high = jnp.where(names > 0, word, 0)
+    for k in (1, 2, 4, 8, 16):
+        inside = number + k < 32
+        low = jnp.where(inside, jnp.minimum(low, pltpu.roll(low, 128 - k, 1)), low)
+        high = jnp.where(inside, jnp.maximum(high, pltpu.roll(high, 128 - k, 1)), high)
+    high = jnp.where(high == low, high - (high & 7), high)
+    record = jnp.where(number == 0, low, pltpu.roll(high, 1, 1))
+    for k in range(RING):
+        rec_v[k] = record[k : k + 1]
+    table_v[m] = rec_v[z]
+
+    pl.semaphore_wait(barrier, len(partners) + nmem - 1)
 
     def ring_right(ref, k, s, r, to, me):
         at = lax.rem(me + RING - k, RING)
@@ -143,25 +160,27 @@
                 tok_left(k + 1).start()
             tok_sib(2 * k + 2, tok_place(k + 1)).start()
 
-    for d in range(1, RING):
-        flag_arrival(d).wait_recv()
-    for d in range(XS):
-        stage_v[d] = flags_v[:, lax.rem(x + d, XS)]
-    table_copies = [
-        send(stage_v.at[d], table_v.at[d], fx_s.at[d - 1], fx_r.at[d - 1], x_peer(d)) for d in range(1, XS)
-    ]
-    for copy in table_copies:
-        copy.start()
-    table_v[0] = stage_v[0]
-    flags_to_s = pltpu.make_async_copy(flags_v, flags_s, sm_sem.at[0])
-    flags_to_s.start()
-    for copy in table_copies:
-        copy.wait_recv()
-    table_to_s = pltpu.make_async_copy(table_v, table_s, sm_sem.at[1])
+    def rec_copy(d):
+        return send(
+            rec_v.at[lax.rem(m + d, nmem) // XS], table_v.at[m], rec_s.at[d - 1], rec_r.at[d - 1], mem_peer(d)
+        )
+
+    def rec_start(d, carry):
+        rec_copy(d).start()
+        return carry
+
+    def rec_wait(d, carry):
+        at = table_v.at[lax.rem(m + nmem - d, nmem)]
+        send(at, at, rec_s.at[d - 1], rec_r.at[d - 1], mem_peer(d)).wait_recv()
+        return carry
+
+    lax.fori_loop(1, nmem, rec_start, 0)
+    lax.fori_loop(1, nmem, rec_wait, 0)
+    table_to_s = pltpu.make_async_copy(table_v, table_s, in_sem.at[3])
     table_to_s.start()
+    tok_step(0)
     loads[0].wait()
     table_to_s.wait()
-    tok_step(0)
 
     def kv_copy(d, i):
         return send(kv_send.at[d - 1, i], kv_all.at[d, i], kv_s.at[d - 1, i], kv_r.at[d - 1, i], x_peer(d))
@@ -170,7 +189,8 @@
         zr = lax.rem(z + ring_offset(i) + RING, RING)
         for d in (2, 1, 3, 0):
             for slot in range(2):
-                block = table_s[(XS - d) % XS, zr, 0, slot]
+                words = table_s[zr * XS + lax.rem(x + d, XS), 0, x * 32 + slot]
+                block = lax.shift_right_logical(words, 3)
                 key = mem_v[0, block]
                 value = mem_v[1, block].astype(F32).T.astype(BF16)
                 if d:
@@ -188,8 +208,14 @@
     lax.fori_loop(4, 8, pack, 0)
     tok_step(2)
     tok_step(3)
-    flags_to_s.wait()
     loads[1].wait()
+    loads[2].wait()
+
+    weight_copies = [
+        send(wo_all.at[0], wo_all.at[1], w_s.at[0], w_r.at[0], sibling),
+        send(wo_all.at[0], wo_all.at[2], w_s.at[1], w_r.at[1], across),
+        send(wo_all.at[2], wo_all.at[3], w_s.at[2], w_r.at[2], sibling),
+    ]
 
     for k in range(RING):
         at = tok_place(order[k])
@@ -227,7 +253,6 @@
 
     q_right(0).start()
     q_left(0).start()
-    blocks = keys_v.shape[0] // BLK
     last = (blocks - 1) * BLK
     halo_copies = [
         send(keys_v.at[pl.ds(last, BLK)], halo.at[0], h_s.at[0], h_r.at[0], following),
@@ -235,6 +260,8 @@
     ]
     for copy in halo_copies:
         copy.start()
+    weight_copies[1].start()
+    weight_copies[0].start()
 
     unit = HD ** (-0.5) * 1.4426950408889634
 
@@ -306,7 +333,8 @@
                 keys = kv_all[d, i, 0:2].reshape(2 * BLK, HD)
                 s = jnp.dot(keys, query, preferred_element_type=F32) * unit
                 for slot in range(2):
-                    flag = flags_s[zr, holder, 0, 2 + 2 * j + slot].astype(F32)
+                    words = table_s[zr * XS + x, 0, holder * 32 + slot]
+                    flag = (lax.shift_right_logical(words, j) & 1).astype(F32)
                     one = s[slot * BLK : (slot + 1) * BLK] + (flag - 1.0) * (-NONE)
                     scores.append(one)
                     high = jnp.max(one, axis=0, keepdims=True)
@@ -339,55 +367,67 @@
 
         return carry
 
-    lax.fori_loop(0, 8, attend, 0)
+    lax.fori_loop(0, 6, attend, 0)
+    weight_copies[1].wait_recv()
+    weight_copies[2].start()
+    lax.fori_loop(6, 8, attend, 0)
     merge(6)
 
     share = 1.0 / (1.0 + jnp.exp(jnp.full((1, HD), -gate_ref[0], F32)))
     share = share[:, 0:1]
-    attended = (share * far_v[...] + (1.0 - share) * near_v[...]).T.astype(BF16)
-    loads[2].wait()
+    att_v[...] = (share * far_v[...] + (1.0 - share) * near_v[...]).T
+
+    def rows_for(where, core):
+        ahead = 1 - 2 * core
+        picked = []
+        for o in (2, 1, 0, -1):
+            chip = lax.rem(where + o * ahead + 2 * RING, RING)
+            picked.append(att_v[pl.ds(pl.multiple_of((chip * 2 + core) * rows, 8), rows), :])
+        return jnp.concatenate(picked, axis=0).astype(BF16)
+
+    att_copies = [
+        send(att_send.at[0], att_all.at[2], a_s.at[0], a_r.at[0], across),
+        send(att_send.at[1], att_all.at[3], a_s.at[1], a_r.at[1], across_other),
+        send(att_send.at[2], att_all.at[1], a_s.at[2], a_r.at[2], sibling),
+    ]
+    for k, (where, core) in enumerate(((y + 4, c), (y + 4, 1 - c), (y, 1 - c))):
+        att_send[k] = rows_for(where, core)
+        att_copies[k].start()
+    att_all[0] = rows_for(y, c)
+    weight_copies[0].wait_recv()
+    weight_copies[2].wait_recv()
+    for copy in att_copies:
+        copy.wait_recv()
+    attended = jnp.concatenate([att_all[k] for k in range(4)], axis=1)
     width = 256
 
     def project_out(n, carry):
         at_left = pl.multiple_of(n * width, width)
         at_right = pl.multiple_of(half + n * width, width)
-        left = jnp.dot(attended, wo_v[:, pl.ds(at_left, width)], preferred_element_type=F32)
-        right = jnp.dot(attended, wo_v[:, pl.ds(at_right, width)], preferred_element_type=F32)
-        for k in range(2 * RING):
+
+        def columns(at):
+            weights = jnp.concatenate([wo_all[k, :, pl.ds(at, width)] for k in range(4)], axis=0)
+            return jnp.dot(attended, weights, preferred_element_type=F32)
+
+        left, right = columns(at_left), columns(at_right)
+        for k in range(4):
             part[k, :, pl.ds(at_left, width)] = jnp.concatenate(
                 [left[k * rows : (k + 1) * rows], right[k * rows : (k + 1) * rows]], axis=0
-            ).astype(BF16)
+            )
         return carry
 
     lax.fori_loop(0, half // width, project_out, 0)
 
-    def y_place(i):
-        return lax.rem(y + ring_offset(i) + RING, RING)
-
-    def part_copy(i):
-        return send(part.at[2 * y_place(i) + 1 - c], sib_part.at[i], ps_s.at[i], ps_r.at[i], sibling)
-
-    for i in range(RING):
-        part_copy(i).start()
-
-    def y_copy(i):
-        return send(y_send.at[i], y_recv.at[i], y_s.at[i], y_r.at[i], y_up if i % 2 == 0 else y_down)
-
-    for i in range(RING):
-        part_copy(i).wait_recv()
-        total = part[2 * y_place(i) + c].astype(F32) + sib_part[i].astype(F32)
-        if i >= 2:
-            y_copy(i - 2).wait_recv()
-            total = total + y_recv[i - 2].astype(F32)
-        if i < 7:
-            y_send[i] = total.astype(BF16)
-            y_copy(i).start()
-        else:
-            y_copy(6).wait_recv()
-            total = total + y_recv[6].astype(F32)
-            out_ref[...] = jnp.concatenate([total[:rows], total[rows:]], axis=1).astype(BF16)
-
-    for copy in flag_copies + table_copies + halo_copies:
+    ahead, behind = at_y(y + 1 - 2 * c, c), at_y(y - 1 + 2 * c, c)
+    y_copies = [
+        send(y_send.at[k], y_recv.at[k], y_s.at[k], y_r.at[k], behind if k == 2 else ahead) for k in range(3)
+    ]
+    y_send[0] = part[0].astype(BF16)
+    y_copies[0].start()
+    y_send[2] = part[3].astype(BF16)
+    y_copies[2].start()
+
+    for copy in weight_copies + halo_copies + att_copies:
         copy.wait_send()
     for k in range(4):
         tok_right(k).wait_send()
@@ -397,43 +437,38 @@
         q_left(k).wait_send()
     for k in range(RING):
         tok_sib(k, tok_place(order[k])).wait_send()
-        part_copy(k).wait_send()
     for i in range(7):
         for copy in o_copies(i, z_up):
             copy.wait_send()
-        y_copy(i).wait_send()
+
+    def rec_sent(d, carry):
+        rec_copy(d).wait_send()
+        return carry
 
     def kv_sent(i, carry):
         for d in range(1, XS):
             kv_copy(d, i).wait_send()
         return carry
 
+    lax.fori_loop(1, nmem, rec_sent, 0)
     lax.fori_loop(0, 8, kv_sent, 0)
 
-
-def requests(retrieved, block_home, owners, blocks_per_owner):
-    rows, entries = retrieved.shape
-    every = jnp.arange(block_home.shape[0], dtype=jnp.int32)
-    home = jnp.sum(jnp.where(retrieved[:, :, None] == every, block_home[None, None, :], 0), axis=-1)
-    named = jnp.any(home[:, :, None] == every, axis=1).reshape(rows, owners, blocks_per_owner)
-    local_id = jnp.arange(blocks_per_owner, dtype=jnp.int32)
-    anyone = jnp.any(named, axis=0)
-    first = jnp.min(jnp.where(anyone, local_id, blocks_per_owner - 1), axis=-1)
-    second = jnp.max(jnp.where(anyone, local_id, 0), axis=-1)
-    of_first = jnp.any(named & (local_id == first[:, None]), axis=-1)
-    of_second = jnp.any(named & (local_id == second[:, None]), axis=-1) & (second != first)
-    flags = jnp.stack([of_first, of_second], axis=-1).astype(jnp.int32)
-    flags = jnp.transpose(flags, (1, 0, 2)).reshape(owners, 2 * rows)
-    record = jnp.concatenate([first[:, None], second[:, None], flags], axis=1)
-    record = jnp.pad(record, ((0, 0), (0, 128 - record.shape[1])))
-    return record.reshape(RING, XS, 1, 128)
+    y_copies[0].wait_recv()
+    y_send[1] = (part[1] + y_recv[0].astype(F32)).astype(BF16)
+    y_copies[1].start()
+    y_copies[2].wait_recv()
+    total = part[2] + y_recv[2].astype(F32)
+    y_copies[1].wait_recv()
+    total = total + y_recv[1].astype(F32)
+    out_ref[...] = jnp.concatenate([total[:rows], total[rows:]], axis=1).astype(BF16)
+    for copy in y_copies:
+        copy.wait_send()
 
 
 def local(tokens, input_weight, output_weight, gate_logit, memory, retrieved, block_home):
     rows, width = tokens.shape
     store = memory.reshape(2, memory.shape[1] // BLK, BLK, HD)
     span = rows * 2 * RING
-    record = requests(retrieved, block_home, RING * XS, memory.shape[1] // BLK)
     vmem = pltpu.VMEM
     dma = pltpu.SemaphoreType.DMA
     packed = (2 * rows, width // 2)
@@ -441,13 +476,11 @@
         vmem((RING, 2) + packed, BF16),
         vmem((span, width), BF16),
         vmem(input_weight.shape, BF16),
-        vmem(output_weight.shape, BF16),
+        vmem((4,) + output_weight.shape, BF16),
         vmem(store.shape, BF16),
-        vmem((RING, XS, 1, 128), jnp.int32),
-        vmem((XS, RING, 1, 128), jnp.int32),
-        vmem((XS, RING, 1, 128), jnp.int32),
-        pltpu.SMEM((RING, XS, 1, 128), jnp.int32),
-        pltpu.SMEM((XS, RING, 1, 128), jnp.int32),
+        vmem((RING, 1, 128), jnp.int32),
+        vmem((RING * XS, 1, 128), jnp.int32),
+        pltpu.SMEM((RING * XS, 1, 128), jnp.int32),
         vmem((XS - 1, RING, 4, BLK, HD), BF16),
         vmem((XS, RING, 4, BLK, HD), BF16),
         vmem((RING, HD, span), BF16),
@@ -461,28 +494,31 @@
         vmem((7, HD, span), BF16),
         vmem((7, 8, span), F32),
         vmem((7, 8, span), F32),
-        vmem((2 * RING,) + packed, BF16),
-        vmem((RING,) + packed, BF16),
-        vmem((7,) + packed, BF16),
-        vmem((7,) + packed, BF16),
-        dma((3,)),
-        dma((4,)), dma((4,)), dma((3,)), dma((3,)), dma((8,)), dma((8,)),
-        dma((7,)), dma((7,)), dma((3,)), dma((3,)), dma((2,)),
+        vmem((span, HD), F32),
+        vmem((3, 4 * rows, HD), BF16),
+        vmem((4, 4 * rows, HD), BF16),
+        vmem((4,) + packed, F32),
+        vmem((3,) + packed, BF16),
+        vmem((3,) + packed, BF16),
+        dma((4,)),
+        dma((4,)), dma((4,)), dma((3,)), dma((3,)), dma((8,)), dma((8,)), dma((31,)), dma((31,)),
         dma((3, 8)), dma((3, 8)), dma((4,)), dma((4,)), dma((3,)), dma((3,)), dma((2,)), dma((2,)),
-        dma((7,)), dma((7,)), dma((7,)), dma((7,)), dma((8,)), dma((8,)), dma((7,)), dma((7,)),
+        dma((7,)), dma((7,)), dma((7,)), dma((7,)),
+        dma((3,)), dma((3,)), dma((3,)), dma((3,)), dma((3,)), dma((3,)),
     ]
     whole = pl.BlockSpec(memory_space=pltpu.VMEM)
     outside = pl.BlockSpec(memory_space=pl.ANY)
+    scalars = pl.BlockSpec(memory_space=pltpu.SMEM)
     return pl.pallas_call(
         kernel,
         out_shape=jax.ShapeDtypeStruct(tokens.shape, BF16),
-        in_specs=[whole, whole, pl.BlockSpec(memory_space=pltpu.SMEM), outside, outside, outside],
+        in_specs=[scalars, scalars, scalars, whole, outside, outside, outside],
         out_specs=whole,
         scratch_shapes=scratch,
         compiler_params=pltpu.CompilerParams(
             collective_id=0, has_side_effects=True, vmem_limit_bytes=56 * 2**20
         ),
-    )(tokens, record, gate_logit, input_weight, output_weight, store)
+    )(retrieved, block_home, gate_logit, tokens, input_weight, output_weight, store)
 
 
 def solution(mesh):

time: 115 us -> 108 us (0.939)
  the two profiles are of different devices: /device:TPU:2 before, /device:TPU:18 now
where the time goes in v2:
time: 108 us
  Pallas kernels  106 us (98%)
  local copies, waits for them, and re-layouts  1.56 us (1%)
    pallas_call x1, Pallas kernels, local(): pl.pallas_call(kernel, out_shape=jax.ShapeDtypeStruct(tokens.shape, BF16)...  106 us

profile of v2, /device:TPU:18, one launch (start us, length us, event | category | flops | bytes accessed | tf_op | source)
XLA Modules:
  0.0 108.0 jit_solution(11302922927714365191)
XLA Ops:
  0.7 105.8 %shard_map.73 = bf16[24,2560]{1,0:T(8,128)(2,1)} custom-call(s32[3,16]{1,0:T(4,128)} %ret_ref.1, s32[1024]{0:T(1024)} %home_ref.1, f32[1]{0:T(128)S(6)} %copy.9.gate_ref, bf16[24,2560]{1,0:T(8,128)(2,1)} %tok_ref.1, bf16[2560,384]{1,0:T(8,128)(2,1)} %wi_hbm.1, bf16[128,2560]{1,0:T(8,128)(2,1)} %wo_hbm.1, bf16[2,32,128,128]{3,2,1,0:T(8,128)(2,1)} %bitcast.1), custom_call_target="tpu_custom_call" | custom-call | tf_op jit(solution)/shard_map/pallas_call | solution.py:512
  106.4 1.6 %copy.10 = bf16[24,2560]{1,0:T(8,128)(2,1)} copy(bf16[24,2560]{1,0:T(8,128)(2,1)} %shard_map.73) | data formatting | bytes 245760
